TPU v7x, 32 devices: a whole 2x2x4 slice. The times are simulated.
32 devices in a mesh: wind: 2 (over y), gx: 4 (over z), gy: 2 (over x), gz: 2 (over core).
Axes of the slice: x: 2, y: 2, z: 4, core: 2. Of those that a mesh axis runs over, the one named last changes fastest.
Arguments:
- pressure: bfloat16 [8192, 8192], P(('wind', 'gx'), ('gy', 'gz')), parts along dimension 0, may hold values from -40 to 40
- fir_taps: bfloat16 [257], replicated, may hold values from -0.375 to 0.375
- influence: bfloat16 [256, 4, 4, 512], P(None, ('gy', 'gz'), 'gx'), may hold values from -0.0625 to 0.0625
- mode_impulse: float32 [256, 64], replicated, may hold values from -0.75 to 0.75
- mode_taps: int32 [256], replicated, may hold values from 1 to 64, as said below
Outputs:
- responses: bfloat16 [512, 4096], P(('wind', 'gx', 'gy', 'gz')), parts along dimension 0
- correlation_score: float32 [512, 4, 4, 512], P('wind', ('gy', 'gz'), 'gx'), parts along dimension 0
There are 2 independent parts, one for each index of `wind`. A program takes and returns all parts, laid end to end along the dimension named above; an argument that names none is the same for every part. Nothing has to cross between parts.
Inputs may be any that keep to these rules, and one draw needn't show every extreme that they name: `mode_taps`: some mode keeps all 64 taps.
All inputs are finite; a program needn't handle non-finite values.
Results may differ from a plain program's by a relative error of at most 0.005.
Values may be sent and summed in bfloat16 or wider, within the bound.
A program may use at most 64 MiB of HBM per device.

v0:
```python
import math
import jax
import jax.numpy as jnp
from jax import lax
from jax.sharding import PartitionSpec as P


def band_matrix(tap_row, row_count):
    tap_count = tap_row.shape[0]
    extended = jnp.concatenate([tap_row[::-1], jnp.zeros((row_count,), tap_row.dtype)])
    tiled_flat = jnp.tile(extended, row_count)[: row_count * (row_count + tap_count - 1)]
    return tiled_flat.reshape(row_count, row_count + tap_count - 1)


def fir_rows(padded_in, tap_row, row_count):
    tap_count = tap_row.shape[0]
    block_rows = min(512, row_count)
    toeplitz = band_matrix(tap_row, block_rows)
    partials = [
        jnp.dot(
            toeplitz,
            padded_in[offset : offset + block_rows + tap_count - 1],
            preferred_element_type=jnp.float32,
        )
        for offset in range(0, row_count, block_rows)
    ]
    return jnp.concatenate(partials, axis=0).astype(jnp.bfloat16)


def dynamic_filter(series, impulse, tap_limits):
    impulse_len = impulse.shape[1]
    kept_mask = jnp.arange(impulse_len, dtype=jnp.int32)[None, :] < tap_limits[:, None]
    kernel_taps = jnp.where(kept_mask, impulse, jnp.zeros_like(impulse))[:, ::-1]
    result = lax.conv_general_dilated(
        series[None],
        kernel_taps[:, None, :],
        window_strides=(1,),
        padding=[(impulse_len - 1, 0)],
        dimension_numbers=("NCH", "OIH", "NCH"),
        feature_group_count=series.shape[0],
        precision=lax.Precision.HIGHEST,
    )
    return result[0]


def score_block(responses, filtered, mean_panel, spread_panel):
    sample_count = filtered.shape[0]
    resp_wide = responses.astype(jnp.float32)
    mean_mode = jnp.mean(resp_wide, axis=1)
    spread_mode = jnp.sqrt(jnp.mean(jnp.square(resp_wide - mean_mode[:, None]), axis=1) + 1e-06)
    cross = jnp.dot(responses, filtered, preferred_element_type=jnp.float32)
    covariance = cross / sample_count - mean_mode[:, None] * mean_panel[None, :]
    return math.sqrt(sample_count) * covariance / (spread_mode[:, None] * spread_panel[None, :])


def body(pressure, fir_taps, influence, mode_impulse, mode_taps):
    tap_count = fir_taps.shape[0]
    regrouped = lax.all_to_all(pressure, "gx", split_axis=1, concat_axis=0, tiled=True)
    zero_rim = jnp.zeros((tap_count - 1, regrouped.shape[1]), regrouped.dtype)
    filtered = fir_rows(
        jnp.concatenate([zero_rim, regrouped], axis=0), fir_taps, regrouped.shape[0]
    )
    lines = influence.reshape(influence.shape[0], -1)
    mode_count = lines.shape[0]
    per_device = mode_count // lax.axis_size(("gx", "gy", "gz"))
    mean_panel = jnp.mean(filtered, axis=0, dtype=jnp.float32)
    spread_panel = jnp.sqrt(
        jnp.mean(jnp.square(filtered.astype(jnp.float32) - mean_panel[None, :]), axis=0) + 1e-06
    )
    first_mode = lax.axis_index(("gx", "gy", "gz")) * per_device
    own_loads = lax.psum_scatter(
        lax.dot_general(
            lines, filtered, (((1,), (1,)), ((), ())), preferred_element_type=jnp.float32
        ),
        ("gx", "gy", "gz"),
        scatter_dimension=0,
        tiled=True,
    )
    own_impulse = lax.dynamic_slice_in_dim(mode_impulse, first_mode, per_device, 0)
    own_limits = lax.dynamic_slice_in_dim(mode_taps, first_mode, per_device, 0)
    own_modes = dynamic_filter(own_loads, own_impulse, own_limits).astype(jnp.bfloat16)
    scores = score_block(
        lax.all_gather(own_modes, ("gx", "gy", "gz"), axis=0, tiled=True),
        filtered,
        mean_panel,
        spread_panel,
    )
    return (own_modes, scores.reshape(influence.shape))


def solution(mesh):
    return jax.shard_map(
        body,
        mesh=mesh,
        in_specs=(
            P(("wind", "gx"), ("gy", "gz")),
            P(),
            P(None, ("gy", "gz"), "gx", None),
            P(),
            P(),
        ),
        out_specs=(P(("wind", "gx", "gy", "gz"), None), P("wind", ("gy", "gz"), "gx", None)),
        check_vma=False,
    )
```

profile of v0, /device:TPU:0, one launch (start us, length us, event | category | flops | bytes accessed | tf_op | source)
XLA Modules:
  0.0 279.5 jit_solution(2012428702665789185)
XLA Ops:
  7.2 6.5 %copy.44 = bf16[1024,2048]{0,1:T(8,128)(2,1)} copy(bf16[1024,2048]{1,0:T(8,128)(2,1)} %param.5) | data formatting | bytes 8388608 | tf_op args[0]
  13.7 6.4 %all-to-all-start = ((bf16[1024,4,512]{0,2,1:T(8,128)(2,1)}), bf16[1024,4,512]{0,2,1:T(8,128)(2,1)}, u32[]{:S(2)}, u32[]{:S(2)}) async-start(bf16[1024,4,512]{0,2,1:T(8,128)(2,1)} %bitcast.53), calls=%async_computation | async-start | bytes 8388608 | tf_op jit(solution)/shard_map/all_to_all | solution.py:58
  20.4 1.3 tile.10
  21.8 0.7 reshape.35
  22.5 91.1 %all-to-all-done = bf16[1024,4,512]{0,2,1:T(8,128)(2,1)} async-done(((bf16[1024,4,512]{0,2,1:T(8,128)(2,1)}), bf16[1024,4,512]{0,2,1:T(8,128)(2,1)}, u32[]{:S(2)}, u32[]{:S(2)}) %all-to-all-start) | async-done | bytes 4194336 | tf_op jit(solution)/shard_map/all_to_all | solution.py:58
  113.6 6.2 %copy.45 = bf16[4,1024,512]{2,1,0:T(8,128)(2,1)} copy(bf16[4,1024,512]{1,2,0:T(8,128)(2,1)} %bitcast.1) | data formatting | bytes 8388608 | tf_op jit(solution)/shard_map/all_to_all | solution.py:58
  119.8 1.7 fusion.18
  121.5 0.6 copy-done.4
  122.1 0.6 fusion.17
  122.7 0.6 fusion.16
  123.3 0.6 fusion.15
  123.9 0.6 fusion.14
  124.4 0.6 fusion.13
  125.0 0.6 fusion.12
  125.6 0.6 fusion.11
  126.2 1.9 copy-done.1
  128.1 3.2 %convolution_bitcast_fusion = f32[256,4096]{0,1:T(8,128)} fusion(bf16[4096,512]{1,0:T(8,128)(2,1)S(1)} %fusion.11, bf16[256,1,1,512]{3,0,2,1:T(8,128)(2,1)S(1)} %copy-done), kind=kOutput, calls=%fused_computation.4 | convolution fusion | flops 1073741824 | bytes 8650752 | tf_op jit(solution)/shard_map/dot_general | solution.py:72
  131.3 5.6 %copy.56 = f32[256,4096]{1,0:T(8,128)} copy(f32[256,4096]{0,1:T(8,128)} %convolution_bitcast_fusion) | data formatting | bytes 8388608
  137.9 70.8 %reduce-scatter.4.cloned.1.call-done = f32[16,4096]{1,0:T(8,128)} async-done(((f32[256,4096]{1,0:T(8,128)}), f32[16,4096]{1,0:T(8,128)}) %reduce-scatter.4.cloned.1.call-update) | async-done | bytes 262160
  208.7 1.5 copy.57
  210.5 0.4 copy.48
  211.0 10.8 %fusion.5 = bf16[8,520,16]{2,0,1:T(8,128)(2,1)S(1)} fusion(f32[16,1,64]{0,1,2:T(1,128)S(1)} %bitcast.64, f32[16,1,7,63]{0,2,3,1:T(8,128)S(1)} %slice.46, f32[16,1,8,520]{0,2,3,1:T(8,128)S(1)} %copy.48), kind=kOutput, calls=%fused_computation.12 | convolution fusion | flops 51341952 | bytes 431680 | tf_op jit(solution)/shard_map/conv_general_dilated | solution.py:34
  221.7 0.7 copy.50
  222.7 0.7 slice_bitcast_fusion.1
  223.5 3.0 %convert_reduce_fusion = f32[512]{0:T(512)S(1)} fusion(bf16[4096,512]{1,0:T(8,128)(2,1)} %copy-done.1), kind=kLoop, calls=%fused_computation.1 | loop fusion | flops 4193792 | bytes 4196352 | tf_op jit(solution)/shard_map/reduce_sum | solution.py:66
  226.4 0.5 copy-done.2
  226.9 1.2 fusion.1
  228.1 35.9 %all-gather.3.cloned.1.call-done = bf16[1,256,4096]{2,1,0:T(8,128)(2,1)} async-done(((bf16[1,16,4096]{2,1,0:T(8,128)(2,1)}), bf16[1,256,4096]{2,1,0:T(8,128)(2,1)}) %all-gather.3.cloned.1.call-update) | async-done | bytes 2097168 | tf_op jit(solution)/shard_map/all_gather | solution.py:83
  264.0 2.1 convert_reduce_fusion.1
  266.1 2.3 fusion.3
  268.4 2.9 %fusion.33 = f32[256,1,1,512]{3,0,2,1:T(8,128)S(1)} fusion(bf16[4096,512]{1,0:T(8,128)(2,1)S(1)} %copy-done.3, bf16[1,256,4096]{2,1,0:T(8,128)(2,1)} %all-gather.3.cloned.1.call-done, f32[512]{0:T(512)S(1)} %add_sqrt_fusion, f32[256]{0:T(256)S(1)} %add_sqrt_fusion.1, f32[512]{0:T(512)S(1)} %broadcast_multiply_fusion, f32[256]{0:T(256)S(1)} %broadcast_multiply_fusion.1), kind=kOutput, calls=%fused_computation.40 | convolution fusion | flops 1074528256 | bytes 6821888 | tf_op jit(solution)/shard_map/dot_general | solution.py:51
  271.3 1.3 copy.52
  (36 shorter events, 1.8 us)
Async XLA Ops:
  7.2 120.9 %copy-start = (bf16[256,1,1,512]{3,0,2,1:T(8,128)(2,1)S(1)}, bf16[256,1,1,512]{3,0,2,1:T(8,128)(2,1)}, u32[]{:S(2)}) copy-start(bf16[256,1,1,512]{3,0,2,1:T(8,128)(2,1)} %param.7) | copy-start | bytes 786436
  13.7 6.5 %copy-start.7 = (bf16[257]{0:T(512)(128)(2,1)S(1)}, bf16[257]{0:T(512)(128)(2,1)}, u32[]{:S(2)}) copy-start(bf16[257]{0:T(512)(128)(2,1)} %param.6) | copy-start | bytes 1546
  13.7 99.9 %all-to-all-start = ((bf16[1024,4,512]{0,2,1:T(8,128)(2,1)}), bf16[1024,4,512]{0,2,1:T(8,128)(2,1)}, u32[]{:S(2)}, u32[]{:S(2)}) async-start(bf16[1024,4,512]{0,2,1:T(8,128)(2,1)} %bitcast.53), calls=%async_computation | async-start | bytes 8388608 | tf_op jit(solution)/shard_map/all_to_all | solution.py:58
  20.1 188.6 %reduce-scatter.4.cloned.1.call-start = ((), (), s32[]{:S(2)}) async-start(), calls=%async_computation.3 | async-start | bytes 4456448
  119.8 2.3 copy-start.4
  126.2 1.9 copy-start.1
  137.0 0.7 copy-start.8
  137.0 0.9 copy-start.5
  137.0 127.0 %all-gather.3.cloned.1.call-start = ((), (), s32[]{:S(2)}) async-start(), calls=%async_computation.2 | async-start | bytes 2228224 | tf_op jit(solution)/shard_map/all_gather | solution.py:83
  210.9 11.5 %copy-start.6 = (pred[8,520]{1,0:T(8,128)(4,1)S(1)}, pred[8,520]{1,0:T(8,128)(4,1)}, u32[]{:S(2)}) copy-start(pred[8,520]{1,0:T(8,128)(4,1)} %constant.52) | copy-start | bytes 12484
  223.4 3.5 %copy-start.2 = (bf16[4096,512]{1,0:T(8,128)(2,1)S(1)}, bf16[4096,512]{1,0:T(8,128)(2,1)}, u32[]{:S(2)}) copy-start(bf16[4096,512]{1,0:T(8,128)(2,1)} %copy-done.1) | copy-start | bytes 12582916
  264.0 4.4 %copy-start.3 = (bf16[4096,512]{1,0:T(8,128)(2,1)S(1)}, bf16[4096,512]{1,0:T(8,128)(2,1)}, u32[]{:S(2)}) copy-start(bf16[4096,512]{1,0:T(8,128)(2,1)} %copy-done.1) | copy-start | bytes 12582916
Sparse Core Ops, SparseCore 0:
  137.1 71.5 reduce-scatter.3
  223.6 40.3 all-gather.2
where the time goes:
time: 280 us
  waiting for transfers between devices  198 us (71%)
  local copies, waits for them, and re-layouts  29.5 us (11%)
  matrix products  22.6 us (8%)
  between operations  14.2 us (5%)
  other arithmetic  8.64 us (3%)
  starting transfers between devices  6.67 us (2%)
    all_to_all x1, waiting for transfers between devices, body(): lax.all_to_all(pressure, 'gx', split_axis=1, concat_axis=0, tiled=True)  91.1 us
    unnamed x3, waiting for transfers between devices  70.8 us
    all_gather x1, waiting for transfers between devices, body(): lax.all_gather(own_modes, ('gx', 'gy', 'gz'), axis=0, tiled=True)  35.9 us
    unnamed x24, local copies, waits for them, and re-layouts  18.8 us
    conv_general_dilated x1, matrix products, dynamic_filter(): lax.conv_general_dilated(series[None], kernel_taps[:, None, :], window_st...  10.8 us
    all_to_all x1, starting transfers between devices, body(): lax.all_to_all(pressure, 'gx', split_axis=1, concat_axis=0, tiled=True)  6.45 us
    all_to_all x1, local copies, waits for them, and re-layouts, body(): lax.all_to_all(pressure, 'gx', split_axis=1, concat_axis=0, tiled=True)  6.23 us
    dot_general x8, matrix products, fir_rows(): jnp.dot(toeplitz, padded_in[offset:offset + block_rows + tap_count - 1],...  5.71 us
  transfers between devices with their start and end apart: 3, of which 3 were waited for; matrix products, arithmetic and copies ran while one was open for 2% of the time, Pallas kernels for 0%

commit v1 on v0

--- a/solution.py
+++ b/solution.py
@@ -3,6 +3,28 @@
 import jax.numpy as jnp
 from jax import lax
 from jax.sharding import PartitionSpec as P
+
+
+def joined_along(blocks, dim):
+    blocks = jnp.moveaxis(blocks, 0, dim)
+    dims = blocks.shape
+    return blocks.reshape(*dims[:dim], dims[dim] * dims[dim + 1], *dims[dim + 2 :])
+
+
+def collect(x, axis, dim):
+    size = lax.axis_size(axis)
+    pairs = [(i, (i + 1) % size) for i in range(size)]
+    back = [(b, a) for a, b in pairs]
+    lower, upper = ([], [])
+    for turn in range(size - 1):
+        if turn % 2 == 0:
+            lower.append(lax.ppermute(lower[-1] if lower else x, axis, pairs))
+        else:
+            upper.append(lax.ppermute(upper[-1] if upper else x, axis, back))
+    tiles = jnp.stack([*lower[::-1], x, *upper])
+    shift = lax.axis_index(axis) - len(lower)
+    tiles = tiles[(jnp.arange(size) - shift) % size]
+    return joined_along(tiles, dim)
 
 
 def band_matrix(tap_row, row_count):
@@ -80,10 +102,7 @@
     own_limits = lax.dynamic_slice_in_dim(mode_taps, first_mode, per_device, 0)
     own_modes = dynamic_filter(own_loads, own_impulse, own_limits).astype(jnp.bfloat16)
     scores = score_block(
-        lax.all_gather(own_modes, ("gx", "gy", "gz"), axis=0, tiled=True),
-        filtered,
-        mean_panel,
-        spread_panel,
+        collect(own_modes, ("gx", "gy", "gz"), 0), filtered, mean_panel, spread_panel
     )
     return (own_modes, scores.reshape(influence.shape))
 

time: 280 us -> 307 us (1.096)
  starting transfers between devices: 6.67 us -> 38.1 us
  waiting for transfers between devices: 198 us -> 184 us
  local copies, waits for them, and re-layouts: 29.5 us -> 41.7 us
  other arithmetic: 8.64 us -> 5.17 us
    all_gather x1 -> x0, waiting for transfers between devices: 35.9 us -> none  [body(): lax.all_gather(own_modes, ('gx', 'gy', 'gz'), axis=0, tiled=True)]
    ppermute x0 -> x15, starting transfers between devices: none -> 31.6 us  [the longest x7 31.6 us: collect(): upper.append(lax.ppermute(upper[-1] if upper else x, axis, back))]
    ppermute x0 -> x15, waiting for transfers between devices: none -> 21.5 us  [the longest x8 15.1 us: collect(): lower.append(lax.ppermute(lower[-1] if lower else x, axis, pairs))]
    unnamed x24 -> x39, local copies, waits for them, and re-layouts: 18.8 us -> 28.6 us
    unnamed x3 -> x2, waiting for transfers between devices: 70.8 us -> 71.1 us
  transfers between devices with their start and end apart: 3 -> 17, of which waited for: 3 -> 9; matrix products, arithmetic and copies ran while one was open for 2% -> 5% of each run, Pallas kernels for 0% -> 0%
where the time goes in v1:
time: 307 us; the launch traced here: 306 us
  waiting for transfers between devices  184 us (60%)
  local copies, waits for them, and re-layouts  41.7 us (14%)
  starting transfers between devices  38.1 us (12%)
  matrix products  23.2 us (8%)
  between operations  14.3 us (5%)
  other arithmetic  5.17 us (2%)
    all_to_all x1, waiting for transfers between devices, body(): lax.all_to_all(pressure, 'gx', split_axis=1, concat_axis=0, tiled=True)  91.1 us
    unnamed x2, waiting for transfers between devices  71.1 us
    ppermute x7, starting transfers between devices, collect(): upper.append(lax.ppermute(upper[-1] if upper else x, axis, back))  31.6 us
    unnamed x39, local copies, waits for them, and re-layouts  28.6 us
    ppermute x8, waiting for transfers between devices, collect(): lower.append(lax.ppermute(lower[-1] if lower else x, axis, pairs))  15.1 us
    conv_general_dilated x1, matrix products, dynamic_filter(): lax.conv_general_dilated(series[None], kernel_taps[:, None, :], window_st...  10.8 us
    all_to_all x1, starting transfers between devices, body(): lax.all_to_all(pressure, 'gx', split_axis=1, concat_axis=0, tiled=True)  6.45 us
    ppermute x7, waiting for transfers between devices, collect(): upper.append(lax.ppermute(upper[-1] if upper else x, axis, back))  6.38 us
  transfers between devices with their start and end apart: 17, of which 9 were waited for; matrix products, arithmetic and copies ran while one was open for 5% of the time, Pallas kernels for 0%

profile of v1, /device:TPU:0, one launch (start us, length us, event | category | flops | bytes accessed | tf_op | source)
XLA Modules:
  0.0 306.2 jit_solution(4877843184902249684)
XLA Ops:
  7.2 6.5 %copy.44 = bf16[1024,2048]{0,1:T(8,128)(2,1)} copy(bf16[1024,2048]{1,0:T(8,128)(2,1)} %param.5) | data formatting | bytes 8388608 | tf_op args[0]
  13.7 6.4 %all-to-all-start = ((bf16[1024,4,512]{0,2,1:T(8,128)(2,1)}), bf16[1024,4,512]{0,2,1:T(8,128)(2,1)}, u32[]{:S(2)}, u32[]{:S(2)}) async-start(bf16[1024,4,512]{0,2,1:T(8,128)(2,1)} %bitcast.73), calls=%async_computation | async-start | bytes 8388608 | tf_op jit(solution)/shard_map/all_to_all | solution.py:80
  20.4 1.3 tile.10
  22.5 91.1 %all-to-all-done = bf16[1024,4,512]{0,2,1:T(8,128)(2,1)} async-done(((bf16[1024,4,512]{0,2,1:T(8,128)(2,1)}), bf16[1024,4,512]{0,2,1:T(8,128)(2,1)}, u32[]{:S(2)}, u32[]{:S(2)}) %all-to-all-start) | async-done | bytes 4194336 | tf_op jit(solution)/shard_map/all_to_all | solution.py:80
  113.5 6.2 %copy.45 = bf16[4,1024,512]{2,1,0:T(8,128)(2,1)} copy(bf16[4,1024,512]{1,2,0:T(8,128)(2,1)} %bitcast.1) | data formatting | bytes 8388608 | tf_op jit(solution)/shard_map/all_to_all | solution.py:80
  119.8 1.7 fusion.16
  126.1 1.9 copy-done.1
  128.1 3.3 %convolution_bitcast_fusion = f32[256,4096]{0,1:T(8,128)} fusion(bf16[4096,512]{1,0:T(8,128)(2,1)S(1)} %fusion.9, bf16[256,1,1,512]{3,0,2,1:T(8,128)(2,1)S(1)} %copy-done), kind=kOutput, calls=%fused_computation.5 | convolution fusion | flops 1073741824 | bytes 8650752 | tf_op jit(solution)/shard_map/dot_general | solution.py:94
  131.3 5.7 %copy.56 = f32[256,4096]{1,0:T(8,128)} copy(f32[256,4096]{0,1:T(8,128)} %convolution_bitcast_fusion) | data formatting | bytes 8388608
  138.0 71.1 %reduce-scatter.4.cloned.1.call-done = f32[16,4096]{1,0:T(8,128)} async-done(((f32[256,4096]{1,0:T(8,128)}), f32[16,4096]{1,0:T(8,128)}) %reduce-scatter.4.cloned.1.call-update) | async-done | bytes 262160
  209.1 1.5 copy.57
  211.3 10.8 %fusion.5 = bf16[8,520,16]{2,0,1:T(8,128)(2,1)S(1)} fusion(f32[16,1,64]{0,1,2:T(1,128)S(1)} %bitcast.84, f32[16,1,7,63]{0,2,3,1:T(8,128)S(1)} %slice.48, f32[16,1,8,520]{0,2,3,1:T(8,128)S(1)} %copy.48), kind=kOutput, calls=%fused_computation.13 | convolution fusion | flops 51341952 | bytes 431680 | tf_op jit(solution)/shard_map/conv_general_dilated | solution.py:56
  222.1 0.7 copy.50
  223.2 7.1 %collective-permute-done = bf16[16,4096]{1,0:T(8,128)(2,1)S(1)} collective-permute-done((bf16[16,4096]{1,0:T(8,128)(2,1)S(1)}, bf16[16,4096]{1,0:T(8,128)(2,1)S(1)}, u32[]{:S(2)}, u32[]{:S(2)}) %collective-permute-start) | collective-permute-done | bytes 131104 | tf_op jit(solution)/shard_map/ppermute | solution.py:21
  230.2 4.4 %collective-permute-start.8 = (bf16[16,4096]{1,0:T(8,128)(2,1)S(1)}, bf16[16,4096]{1,0:T(8,128)(2,1)S(1)}, u32[]{:S(2)}, u32[]{:S(2)}) collective-permute-start(bf16[16,4096]{1,0:T(8,128)(2,1)S(1)} %slice_bitcast_fusion), channel_id=1, source_target_pairs={{1,0},{2,1},{3,2},{4,3},{5,4},{6,5},{7,6},{8,7},{9,8},{10,9},{11,1... | collective-permute-start | bytes 393224 | tf_op jit(solution)/shard_map/ppermute | solution.py:23
  234.7 2.8 collective-permute-done.1
  237.5 4.4 %collective-permute-start.9 = (bf16[16,4096]{1,0:T(8,128)(2,1)S(1)}, bf16[16,4096]{1,0:T(8,128)(2,1)S(1)}, u32[]{:S(2)}, u32[]{:S(2)}) collective-permute-start(bf16[16,4096]{1,0:T(8,128)(2,1)S(1)} %collective-permute-done.8), channel_id=1, source_target_pairs={{1,0},{2,1},{3,2},{4,3},{5,4},{6,5},{7,6},{8,7},{9,8},{10,9},{11,1... | collective-permute-start | bytes 393224 | tf_op jit(solution)/shard_map/ppermute | solution.py:23
  241.9 2.7 collective-permute-done.2
  244.7 4.5 %collective-permute-start.10 = (bf16[16,4096]{1,0:T(8,128)(2,1)S(1)}, bf16[16,4096]{1,0:T(8,128)(2,1)S(1)}, u32[]{:S(2)}, u32[]{:S(2)}) collective-permute-start(bf16[16,4096]{1,0:T(8,128)(2,1)S(1)} %collective-permute-done.9), channel_id=1, source_target_pairs={{1,0},{2,1},{3,2},{4,3},{5,4},{6,5},{7,6},{8,7},{9,8},{10,9},{11,1... | collective-permute-start | bytes 393224 | tf_op jit(solution)/shard_map/ppermute | solution.py:23
  249.2 2.6 collective-permute-done.3
  251.7 2.8 convert_reduce_fusion
  254.5 4.5 %collective-permute-start.11 = (bf16[16,4096]{1,0:T(8,128)(2,1)S(1)}, bf16[16,4096]{1,0:T(8,128)(2,1)S(1)}, u32[]{:S(2)}, u32[]{:S(2)}) collective-permute-start(bf16[16,4096]{1,0:T(8,128)(2,1)S(1)} %collective-permute-done.10), channel_id=1, source_target_pairs={{1,0},{2,1},{3,2},{4,3},{5,4},{6,5},{7,6},{8,7},{9,8},{10,9},{11,1... | collective-permute-start | bytes 393224 | tf_op jit(solution)/shard_map/ppermute | solution.py:23
  259.0 2.5 collective-permute-done.11
  261.6 4.6 %collective-permute-start.12 = (bf16[16,4096]{1,0:T(8,128)(2,1)S(1)}, bf16[16,4096]{1,0:T(8,128)(2,1)S(1)}, u32[]{:S(2)}, u32[]{:S(2)}) collective-permute-start(bf16[16,4096]{1,0:T(8,128)(2,1)S(1)} %collective-permute-done.11), channel_id=1, source_target_pairs={{1,0},{2,1},{3,2},{4,3},{5,4},{6,5},{7,6},{8,7},{9,8},{10,9},{11,1... | collective-permute-start | bytes 393224 | tf_op jit(solution)/shard_map/ppermute | solution.py:23
  266.1 1.2 fusion.1
  267.3 1.4 collective-permute-done.12
  268.6 4.6 %collective-permute-start.13 = (bf16[16,4096]{1,0:T(8,128)(2,1)S(1)}, bf16[16,4096]{1,0:T(8,128)(2,1)S(1)}, u32[]{:S(2)}, u32[]{:S(2)}) collective-permute-start(bf16[16,4096]{1,0:T(8,128)(2,1)S(1)} %collective-permute-done.12), channel_id=1, source_target_pairs={{1,0},{2,1},{3,2},{4,3},{5,4},{6,5},{7,6},{8,7},{9,8},{10,9},{11,1... | collective-permute-start | bytes 393224 | tf_op jit(solution)/shard_map/ppermute | solution.py:23
  273.2 2.5 collective-permute-done.13
  275.7 4.6 %collective-permute-start.14 = (bf16[16,4096]{1,0:T(8,128)(2,1)S(1)}, bf16[16,4096]{1,0:T(8,128)(2,1)S(1)}, u32[]{:S(2)}, u32[]{:S(2)}) collective-permute-start(bf16[16,4096]{1,0:T(8,128)(2,1)S(1)} %collective-permute-done.13), channel_id=1, source_target_pairs={{1,0},{2,1},{3,2},{4,3},{5,4},{6,5},{7,6},{8,7},{9,8},{10,9},{11,1... | collective-permute-start | bytes 393224 | tf_op jit(solution)/shard_map/ppermute | solution.py:23
  291.0 2.3 gather_fusion
  294.6 3.5 %fusion.22 = f32[256,1,1,512]{3,0,2,1:T(8,128)S(1)} fusion(bf16[256,4096]{1,0:T(8,128)(2,1)S(1)} %bitcast.72, bf16[4096,512]{1,0:T(8,128)(2,1)} %copy-done.1, f32[512]{0:T(512)S(1)} %add_sqrt_fusion.1, f32[256]{0:T(256)S(1)} %sqrt.18, f32[512]{0:T(512)S(1)} %broadcast_multiply_fusion.1, f32[256]{0:T(256)S(1)} %div.26), kind=kOutput, calls=%fused_computation.39 | convolution fusion | flops 1074528256 | bytes 6821888 | tf_op jit(solution)/shard_map/dot_general | solution.py:73
  298.0 1.3 copy.52
  (84 shorter events, 19.5 us)
Async XLA Ops:
  7.2 120.9 %copy-start = (bf16[256,1,1,512]{3,0,2,1:T(8,128)(2,1)S(1)}, bf16[256,1,1,512]{3,0,2,1:T(8,128)(2,1)}, u32[]{:S(2)}) copy-start(bf16[256,1,1,512]{3,0,2,1:T(8,128)(2,1)} %param.7) | copy-start | bytes 786436
  13.6 6.5 %copy-start.7 = (bf16[257]{0:T(512)(128)(2,1)S(1)}, bf16[257]{0:T(512)(128)(2,1)}, u32[]{:S(2)}) copy-start(bf16[257]{0:T(512)(128)(2,1)} %param.6) | copy-start | bytes 1546
  13.7 99.9 %all-to-all-start = ((bf16[1024,4,512]{0,2,1:T(8,128)(2,1)}), bf16[1024,4,512]{0,2,1:T(8,128)(2,1)}, u32[]{:S(2)}, u32[]{:S(2)}) async-start(bf16[1024,4,512]{0,2,1:T(8,128)(2,1)} %bitcast.73), calls=%async_computation | async-start | bytes 8388608 | tf_op jit(solution)/shard_map/all_to_all | solution.py:80
  20.1 189.0 %reduce-scatter.4.cloned.1.call-start = ((), (), s32[]{:S(2)}) async-start(), calls=%async_computation.2 | async-start | bytes 4456448
  119.8 2.3 copy-start.3
  126.1 1.9 copy-start.1
  137.0 0.7 copy-start.8
  137.0 0.9 copy-start.5
  211.3 11.5 %copy-start.6 = (pred[8,520]{1,0:T(8,128)(4,1)S(1)}, pred[8,520]{1,0:T(8,128)(4,1)}, u32[]{:S(2)}) copy-start(pred[8,520]{1,0:T(8,128)(4,1)} %constant.69) | copy-start | bytes 12484
  223.1 44.2 %copy-start.4 = (bf16[16,4096]{1,0:T(8,128)(2,1)}, bf16[16,4096]{1,0:T(8,128)(2,1)S(1)}, u32[]{:S(2)}) copy-start(bf16[16,4096]{1,0:T(8,128)(2,1)S(1)} %slice_bitcast_fusion) | copy-start | bytes 393220
  223.1 7.1 %collective-permute-start = (bf16[16,4096]{1,0:T(8,128)(2,1)S(1)}, bf16[16,4096]{1,0:T(8,128)(2,1)S(1)}, u32[]{:S(2)}, u32[]{:S(2)}) collective-permute-start(bf16[16,4096]{1,0:T(8,128)(2,1)S(1)} %slice_bitcast_fusion), channel_id=1, source_target_pairs={{0,1},{1,2},{2,3},{3,4},{4,5},{5,6},{6,7},{7,8},{8,9},{9,10},{10,1... | collective-permute-start | bytes 393224 | tf_op jit(solution)/shard_map/ppermute | solution.py:21
  230.2 7.2 %collective-permute-start.1 = (bf16[16,4096]{1,0:T(8,128)(2,1)S(1)}, bf16[16,4096]{1,0:T(8,128)(2,1)S(1)}, u32[]{:S(2)}, u32[]{:S(2)}) collective-permute-start(bf16[16,4096]{1,0:T(8,128)(2,1)S(1)} %collective-permute-done), channel_id=1, source_target_pairs={{0,1},{1,2},{2,3},{3,4},{4,5},{5,6},{6,7},{7,8},{8,9},{9,10},{10,1... | collective-permute-start | bytes 393224 | tf_op jit(solution)/shard_map/ppermute | solution.py:21
  230.2 7.2 %collective-permute-start.8 = (bf16[16,4096]{1,0:T(8,128)(2,1)S(1)}, bf16[16,4096]{1,0:T(8,128)(2,1)S(1)}, u32[]{:S(2)}, u32[]{:S(2)}) collective-permute-start(bf16[16,4096]{1,0:T(8,128)(2,1)S(1)} %slice_bitcast_fusion), channel_id=1, source_target_pairs={{1,0},{2,1},{3,2},{4,3},{5,4},{6,5},{7,6},{8,7},{9,8},{10,9},{11,1... | collective-permute-start | bytes 393224 | tf_op jit(solution)/shard_map/ppermute | solution.py:23
  237.4 7.2 %collective-permute-start.2 = (bf16[16,4096]{1,0:T(8,128)(2,1)S(1)}, bf16[16,4096]{1,0:T(8,128)(2,1)S(1)}, u32[]{:S(2)}, u32[]{:S(2)}) collective-permute-start(bf16[16,4096]{1,0:T(8,128)(2,1)S(1)} %collective-permute-done.1), channel_id=1, source_target_pairs={{0,1},{1,2},{2,3},{3,4},{4,5},{5,6},{6,7},{7,8},{8,9},{9,10},{10,1... | collective-permute-start | bytes 393224 | tf_op jit(solution)/shard_map/ppermute | solution.py:21
  237.4 28.7 %copy-start.2 = (bf16[4096,512]{1,0:T(8,128)(2,1)S(1)}, bf16[4096,512]{1,0:T(8,128)(2,1)}, u32[]{:S(2)}) copy-start(bf16[4096,512]{1,0:T(8,128)(2,1)} %copy-done.1) | copy-start | bytes 12582916
  237.5 7.2 %collective-permute-start.9 = (bf16[16,4096]{1,0:T(8,128)(2,1)S(1)}, bf16[16,4096]{1,0:T(8,128)(2,1)S(1)}, u32[]{:S(2)}, u32[]{:S(2)}) collective-permute-start(bf16[16,4096]{1,0:T(8,128)(2,1)S(1)} %collective-permute-done.8), channel_id=1, source_target_pairs={{1,0},{2,1},{3,2},{4,3},{5,4},{6,5},{7,6},{8,7},{9,8},{10,9},{11,1... | collective-permute-start | bytes 393224 | tf_op jit(solution)/shard_map/ppermute | solution.py:23
  244.6 7.1 %collective-permute-start.3 = (bf16[16,4096]{1,0:T(8,128)(2,1)S(1)}, bf16[16,4096]{1,0:T(8,128)(2,1)S(1)}, u32[]{:S(2)}, u32[]{:S(2)}) collective-permute-start(bf16[16,4096]{1,0:T(8,128)(2,1)S(1)} %collective-permute-done.2), channel_id=1, source_target_pairs={{0,1},{1,2},{2,3},{3,4},{4,5},{5,6},{6,7},{7,8},{8,9},{9,10},{10,1... | collective-permute-start | bytes 393224 | tf_op jit(solution)/shard_map/ppermute | solution.py:21
  244.7 9.9 %collective-permute-start.10 = (bf16[16,4096]{1,0:T(8,128)(2,1)S(1)}, bf16[16,4096]{1,0:T(8,128)(2,1)S(1)}, u32[]{:S(2)}, u32[]{:S(2)}) collective-permute-start(bf16[16,4096]{1,0:T(8,128)(2,1)S(1)} %collective-permute-done.9), channel_id=1, source_target_pairs={{1,0},{2,1},{3,2},{4,3},{5,4},{6,5},{7,6},{8,7},{9,8},{10,9},{11,1... | collective-permute-start | bytes 393224 | tf_op jit(solution)/shard_map/ppermute | solution.py:23
  251.7 7.3 %collective-permute-start.4 = (bf16[16,4096]{1,0:T(8,128)(2,1)S(1)}, bf16[16,4096]{1,0:T(8,128)(2,1)S(1)}, u32[]{:S(2)}, u32[]{:S(2)}) collective-permute-start(bf16[16,4096]{1,0:T(8,128)(2,1)S(1)} %collective-permute-done.3), channel_id=1, source_target_pairs={{0,1},{1,2},{2,3},{3,4},{4,5},{5,6},{6,7},{7,8},{8,9},{9,10},{10,1... | collective-permute-start | bytes 393224 | tf_op jit(solution)/shard_map/ppermute | solution.py:21
  254.5 7.0 %collective-permute-start.11 = (bf16[16,4096]{1,0:T(8,128)(2,1)S(1)}, bf16[16,4096]{1,0:T(8,128)(2,1)S(1)}, u32[]{:S(2)}, u32[]{:S(2)}) collective-permute-start(bf16[16,4096]{1,0:T(8,128)(2,1)S(1)} %collective-permute-done.10), channel_id=1, source_target_pairs={{1,0},{2,1},{3,2},{4,3},{5,4},{6,5},{7,6},{8,7},{9,8},{10,9},{11,1... | collective-permute-start | bytes 393224 | tf_op jit(solution)/shard_map/ppermute | solution.py:23
  259.0 7.1 %collective-permute-start.5 = (bf16[16,4096]{1,0:T(8,128)(2,1)S(1)}, bf16[16,4096]{1,0:T(8,128)(2,1)S(1)}, u32[]{:S(2)}, u32[]{:S(2)}) collective-permute-start(bf16[16,4096]{1,0:T(8,128)(2,1)S(1)} %collective-permute-done.4), channel_id=1, source_target_pairs={{0,1},{1,2},{2,3},{3,4},{4,5},{5,6},{6,7},{7,8},{8,9},{9,10},{10,1... | collective-permute-start | bytes 393224 | tf_op jit(solution)/shard_map/ppermute | solution.py:21
  261.6 7.1 %collective-permute-start.12 = (bf16[16,4096]{1,0:T(8,128)(2,1)S(1)}, bf16[16,4096]{1,0:T(8,128)(2,1)S(1)}, u32[]{:S(2)}, u32[]{:S(2)}) collective-permute-start(bf16[16,4096]{1,0:T(8,128)(2,1)S(1)} %collective-permute-done.11), channel_id=1, source_target_pairs={{1,0},{2,1},{3,2},{4,3},{5,4},{6,5},{7,6},{8,7},{9,8},{10,9},{11,1... | collective-permute-start | bytes 393224 | tf_op jit(solution)/shard_map/ppermute | solution.py:23
  266.1 7.1 %collective-permute-start.6 = (bf16[16,4096]{1,0:T(8,128)(2,1)S(1)}, bf16[16,4096]{1,0:T(8,128)(2,1)S(1)}, u32[]{:S(2)}, u32[]{:S(2)}) collective-permute-start(bf16[16,4096]{1,0:T(8,128)(2,1)S(1)} %collective-permute-done.5), channel_id=1, source_target_pairs={{0,1},{1,2},{2,3},{3,4},{4,5},{5,6},{6,7},{7,8},{8,9},{9,10},{10,1... | collective-permute-start | bytes 393224 | tf_op jit(solution)/shard_map/ppermute | solution.py:21
  268.6 7.1 %collective-permute-start.13 = (bf16[16,4096]{1,0:T(8,128)(2,1)S(1)}, bf16[16,4096]{1,0:T(8,128)(2,1)S(1)}, u32[]{:S(2)}, u32[]{:S(2)}) collective-permute-start(bf16[16,4096]{1,0:T(8,128)(2,1)S(1)} %collective-permute-done.12), channel_id=1, source_target_pairs={{1,0},{2,1},{3,2},{4,3},{5,4},{6,5},{7,6},{8,7},{9,8},{10,9},{11,1... | collective-permute-start | bytes 393224 | tf_op jit(solution)/shard_map/ppermute | solution.py:23
  273.2 7.1 %collective-permute-start.7 = (bf16[16,4096]{1,0:T(8,128)(2,1)S(1)}, bf16[16,4096]{1,0:T(8,128)(2,1)S(1)}, u32[]{:S(2)}, u32[]{:S(2)}) collective-permute-start(bf16[16,4096]{1,0:T(8,128)(2,1)S(1)} %collective-permute-done.6), channel_id=1, source_target_pairs={{0,1},{1,2},{2,3},{3,4},{4,5},{5,6},{6,7},{7,8},{8,9},{9,10},{10,1... | collective-permute-start | bytes 393224 | tf_op jit(solution)/shard_map/ppermute | solution.py:21
  275.7 14.6 %collective-permute-start.14 = (bf16[16,4096]{1,0:T(8,128)(2,1)S(1)}, bf16[16,4096]{1,0:T(8,128)(2,1)S(1)}, u32[]{:S(2)}, u32[]{:S(2)}) collective-permute-start(bf16[16,4096]{1,0:T(8,128)(2,1)S(1)} %collective-permute-done.13), channel_id=1, source_target_pairs={{1,0},{2,1},{3,2},{4,3},{5,4},{6,5},{7,6},{8,7},{9,8},{10,9},{11,1... | collective-permute-start | bytes 393224 | tf_op jit(solution)/shard_map/ppermute | solution.py:23
Sparse Core Ops, SparseCore 0:
  137.2 71.8 reduce-scatter.3
